TPU v7x, 32 devices: a whole 2x2x4 slice. The times are simulated.
32 devices in a mesh: outer: 8 (over z, core), inner: 4 (over y, x).
Axes of the slice: x: 2, y: 2, z: 4, core: 2. Of those that a mesh axis runs over, the one named last changes fastest.
Arguments:
- queries: bfloat16 [8, 4096, 128], P(None, ('outer', 'inner')), may hold values from -6 to 6
- key_states: bfloat16 [4096, 128], P(('outer', 'inner')), may hold values from -6 to 6
- value_states: bfloat16 [4096, 128], P(('outer', 'inner')), may hold values from -6 to 6
- outputs: bfloat16 [8, 4096, 128], P(None, ('outer', 'inner')), may hold values from -6 to 6
- grad_outputs: bfloat16 [8, 4096, 128], P(None, ('outer', 'inner')), may hold values from -6 to 6
- log_sums: float32 [8, 4096], P(None, ('outer', 'inner')), may hold values from -1 to 20
- span_order: int32 [64], replicated, may hold values from 0 to 63, as said below
Outputs:
- query_grads: bfloat16 [8, 4096, 128], P(None, ('outer', 'inner'))
- key_grads: bfloat16 [4096, 128], P(('outer', 'inner'))
- value_grads: bfloat16 [4096, 128], P(('outer', 'inner'))
Inputs may be any that keep to these rules, and one draw needn't show every extreme that they name: span_order is a permutation of the 64 position blocks; entries 2 d and 2 d + 1 (the blocks stored on device d) add up to 63.
All inputs are finite; a program needn't handle non-finite values.
Results may differ from a plain program's by a relative error of at most 0.0052.
Values may be sent and summed in bfloat16 or wider, within the bound.
A program may use at most 64 MiB of HBM per device.

v0:
```python
import math

import jax
import jax.numpy as jnp
from jax import lax
from jax.sharding import PartitionSpec as P


def table_lookup(table, indices):
    columns = jnp.arange(table.shape[0], dtype=jnp.int32)
    hits = indices[:, None] == columns[None, :]
    return jnp.sum(jnp.where(hits, table[None, :], 0), axis=1)


def row_positions(table, row_ids, span_rows):
    return table_lookup(table, row_ids // span_rows) * span_rows + row_ids % span_rows


def body(queries, key_states, value_states, outputs, grad_outputs, log_sums, span_order):
    head_count, row_count, head_width = queries.shape
    softmax_scale = 1.0 / math.sqrt(head_width)
    span_rows = row_count // 2
    query_rows = queries.reshape(head_count * row_count, head_width)
    grad_rows = grad_outputs.reshape(head_count * row_count, head_width)
    deltas = jnp.sum(
        grad_outputs.astype(jnp.float32) * outputs.astype(jnp.float32), axis=-1
    ).reshape(head_count * row_count, 1)
    log_norm = log_sums.reshape(head_count * row_count, 1)
    device_rank = lax.axis_index("outer") * lax.axis_size("inner") + lax.axis_index("inner")
    total_rows = row_count * lax.axis_size("outer") * lax.axis_size("inner")
    own_ids = device_rank * row_count + jnp.arange(row_count, dtype=jnp.int32)
    query_pos = row_positions(span_order, own_ids, span_rows)
    query_pos_rows = jnp.tile(query_pos, head_count)
    latest = jnp.max(query_pos)
    initial = (
        jnp.zeros((head_count * row_count, head_width), jnp.float32),
        jnp.zeros((total_rows, 2 * head_width), jnp.float32),
    )
    group_key, group_value = (
        lax.all_gather(key_states, "inner", axis=0, tiled=True),
        lax.all_gather(value_states, "inner", axis=0, tiled=True),
    )
    key_piece = lax.all_gather(group_key, "outer", axis=0, tiled=True)
    value_piece = lax.all_gather(group_value, "outer", axis=0, tiled=True)
    piece_rows = key_piece.shape[0]
    block_rows = 1024

    def one_block(step_index, state):
        local_start = step_index * block_rows
        key_block = lax.dynamic_slice_in_dim(key_piece, local_start, block_rows, 0)
        value_block = lax.dynamic_slice_in_dim(value_piece, local_start, block_rows, 0)
        key_ids = local_start + jnp.arange(block_rows, dtype=jnp.int32)
        key_pos = row_positions(span_order, key_ids, span_rows)

        def compute(inner_state):
            grad_query, grad_keys = inner_state
            scores = (
                jnp.dot(query_rows, key_block.T, preferred_element_type=jnp.float32) * softmax_scale
            )
            visible = query_pos_rows[:, None] >= key_pos[None, :]
            attend = jnp.where(visible, jnp.exp(scores - log_norm), 0.0)
            grad_prob = jnp.dot(grad_rows, value_block.T, preferred_element_type=jnp.float32)
            grad_score = attend * (grad_prob - deltas)
            attend_low = attend.astype(jnp.bfloat16)
            score_low = grad_score.astype(jnp.bfloat16)
            grad_query = (
                grad_query
                + jnp.dot(score_low, key_block, preferred_element_type=jnp.float32) * softmax_scale
            )
            key_part = (
                jnp.dot(score_low.T, query_rows, preferred_element_type=jnp.float32) * softmax_scale
            )
            value_part = jnp.dot(attend_low.T, grad_rows, preferred_element_type=jnp.float32)
            current = lax.dynamic_slice_in_dim(grad_keys, local_start, block_rows, 0)
            updated = current + jnp.concatenate([key_part, value_part], axis=1)
            grad_keys = lax.dynamic_update_slice_in_dim(grad_keys, updated, local_start, 0)
            return (grad_query, grad_keys)

        def unchanged(kept):
            return kept

        return lax.cond(latest >= jnp.min(key_pos), compute, unchanged, state)

    grad_query, grad_keys = lax.fori_loop(0, piece_rows // block_rows, one_block, initial)
    group_part = lax.psum_scatter(grad_keys, "outer", scatter_dimension=0, tiled=True)
    own_grads = lax.psum_scatter(group_part, "inner", scatter_dimension=0, tiled=True)
    query_grads = grad_query.reshape(head_count, row_count, head_width).astype(jnp.bfloat16)
    key_grads = own_grads[:, :head_width].astype(jnp.bfloat16)
    value_grads = own_grads[:, head_width:].astype(jnp.bfloat16)
    return (query_grads, key_grads, value_grads)


def solution(mesh):
    return jax.shard_map(
        body,
        mesh=mesh,
        in_specs=(
            P(None, ("outer", "inner"), None),
            P(("outer", "inner"), None),
            P(("outer", "inner"), None),
            P(None, ("outer", "inner"), None),
            P(None, ("outer", "inner"), None),
            P(None, ("outer", "inner")),
            P(),
        ),
        out_specs=(
            P(None, ("outer", "inner"), None),
            P(("outer", "inner"), None),
            P(("outer", "inner"), None),
        ),
        check_vma=False,
    )
```

profile of v0, /device:TPU:0, one launch (start us, length us, event | category | flops | bytes accessed | tf_op | source)
XLA Modules:
  0.0 190.1 jit_solution(17335582080181287121)
XLA Ops:
  7.3 11.5 %all_gather.12 = bf16[512,128]{1,0:T(8,128)(2,1)} all-gather(bf16[128,128]{1,0:T(8,128)(2,1)} %param.12), channel_id=1, replica_groups=mesh['outer'=8,'inner'=4] {'inner'}, dimensions={0}, use_global_device_ids=true | all-gather | bytes 163840 | tf_op jit(solution)/shard_map/all_gather | solution.py:40
  18.8 8.9 %all_gather.14 = bf16[512,128]{1,0:T(8,128)(2,1)} all-gather(bf16[128,128]{1,0:T(8,128)(2,1)} %param.13), channel_id=1, replica_groups=mesh['outer'=8,'inner'=4] {'inner'}, dimensions={0}, use_global_device_ids=true | all-gather | bytes 163840 | tf_op jit(solution)/shard_map/all_gather | solution.py:41
  27.8 0.7 select_reduce_fusion.1
  28.6 1.2 multiply_reduce_fusion
  29.8 0.6 fusion.27
  30.5 10.8 %all-gather.3.cloned.1.call-done = bf16[4096,128]{1,0:T(8,128)(2,1)} async-done(((bf16[512,128]{1,0:T(8,128)(2,1)}), bf16[4096,128]{1,0:T(8,128)(2,1)}) %all-gather.3.cloned.1.call-update) | async-done | bytes 1048592 | tf_op jit(solution)/shard_map/all_gather | solution.py:43
  41.3 23.4 %all-gather.5.cloned.1.call-done = bf16[4096,128]{1,0:T(8,128)(2,1)} async-done(((bf16[512,128]{1,0:T(8,128)(2,1)}), bf16[4096,128]{1,0:T(8,128)(2,1)}) %all-gather.5.cloned.1.call-update) | async-done | bytes 1048592 | tf_op jit(solution)/shard_map/all_gather | solution.py:44
  64.7 2.2 %broadcast_in_dim.69 = f32[4096,256]{1,0:T(8,128)} broadcast(f32[]{:T(128)} %constant.171.clone.1), dimensions={} | broadcast | bytes 4194308 | tf_op jit(solution)/shard_map/broadcast_in_dim | solution.py:37
  66.9 39.7 %while.18 = (s32[]{:T(128)}, f32[1024,128]{1,0:T(8,128)S(1)}, f32[4096,256]{1,0:T(8,128)}, s32[64]{0:T(128)S(1)}, s32[]{:T(128)}, /*index=5*/bf16[4096,128]{1,0:...) while((s32[]{:T(128)}, f32[1024,128]{1,0:T(8,128)S(1)}, ...), condition=%wide.region_8.9_spmd.clone, body=%wide.region_3.8_spmd.clone.sunk | while | flops 1355905024 | bytes 26006620 | solution.py:84
  67.1 0.7 fusion.37
  69.0 7.8 %conditional.3 = ((f32[1024,128]{1,0:T(8,128)S(1)}, f32[4096,256]{1,0:T(8,128)})) conditional(s32[]{:T(128)} %convert_element_type.47, (f32[1024,128]{1,0:T(8,128)S(1)}, f32[4096,256]{1,0:T(8,128)}) %tuple.68, (s32[128]{0:T(128)S(1)}, s32[1024]{0:T(1024)S(1)}, s32[]{:T(128)}, bf16[4096,128]{1,0:T(8,128)(2,1)S(1)}, bf16[1024,128]{1,0:T(8,128)(2,1)S(1)}, ...), branch_computations={%region_6.6_spmd, %region_7.7_spmd} | conditional | flops 1355677696 | bytes 25985610 | solution.py:82
  69.0 0.7 fusion.11
  69.7 0.9 fusion.4
  70.7 2.3 %fusion.2 = bf16[1024,1024]{0,1:T(8,128)(2,1)S(1)} fusion(f32[1024,1024]{1,0:T(8,128)S(1)} %fusion.11, bf16[1024,128]{1,0:T(8,128)(2,1)S(1)} %get-tuple-element.413, f32[1024]{0:T(1024)S(1)} %bitcast.30, f32[1024]{0:T(1024)S(1)} %bitcast.33, s32[1024]{0:T(1024)S(1)} %broadcast_bitcast_fusion, s32[1024]{0:T(1024)S(1)} %get-tuple-element.407, ...), kind=kOutput, calls=%fused_computation.2 | convolution fusion | flops 275775488 | bytes 6832132 | tf_op jit(solution)/shard_map/while/body/eval_jaxpr/cond/branch_1_fun/dot_general | solution.py:62
  73.0 0.8 fusion.7
  73.8 0.7 convolution_multiply_fusion
  74.5 2.3 %fusion.8 = f32[4096,256]{1,0:T(8,128)} fusion(f32[4096,256]{1,0:T(8,128)} %get-tuple-element.415, s32[]{:T(128)S(6)} %select_n.88, f32[1024,128]{1,0:T(8,128)S(1)} %fusion.4, f32[1024,128]{1,0:T(8,128)S(1)} %convolution_multiply_fusion), kind=kLoop, calls=%fused_computation.11 | loop fusion | flops 524288 | bytes 3145732 | tf_op jit(solution)/shard_map/while/body/eval_jaxpr/cond/branch_1_fun/dynamic_update_slice | solution.py:76
  77.0 0.7 fusion.37
  78.9 7.9 %conditional.3 = ((f32[1024,128]{1,0:T(8,128)S(1)}, f32[4096,256]{1,0:T(8,128)})) conditional(s32[]{:T(128)} %convert_element_type.47, (f32[1024,128]{1,0:T(8,128)S(1)}, f32[4096,256]{1,0:T(8,128)}) %tuple.68, (s32[128]{0:T(128)S(1)}, s32[1024]{0:T(1024)S(1)}, s32[]{:T(128)}, bf16[4096,128]{1,0:T(8,128)(2,1)S(1)}, bf16[1024,128]{1,0:T(8,128)(2,1)S(1)}, ...), branch_computations={%region_6.6_spmd, %region_7.7_spmd} | conditional | flops 1355677696 | bytes 25985610 | solution.py:82
  78.9 0.7 fusion.11
  79.6 0.9 fusion.4
  80.6 2.3 %fusion.2 = bf16[1024,1024]{0,1:T(8,128)(2,1)S(1)} fusion(f32[1024,1024]{1,0:T(8,128)S(1)} %fusion.11, bf16[1024,128]{1,0:T(8,128)(2,1)S(1)} %get-tuple-element.413, f32[1024]{0:T(1024)S(1)} %bitcast.30, f32[1024]{0:T(1024)S(1)} %bitcast.33, s32[1024]{0:T(1024)S(1)} %broadcast_bitcast_fusion, s32[1024]{0:T(1024)S(1)} %get-tuple-element.407, ...), kind=kOutput, calls=%fused_computation.2 | convolution fusion | flops 275775488 | bytes 6832132 | tf_op jit(solution)/shard_map/while/body/eval_jaxpr/cond/branch_1_fun/dot_general | solution.py:62
  82.9 0.8 fusion.7
  83.7 0.7 convolution_multiply_fusion
  84.4 2.4 %fusion.8 = f32[4096,256]{1,0:T(8,128)} fusion(f32[4096,256]{1,0:T(8,128)} %get-tuple-element.415, s32[]{:T(128)S(6)} %select_n.88, f32[1024,128]{1,0:T(8,128)S(1)} %fusion.4, f32[1024,128]{1,0:T(8,128)S(1)} %convolution_multiply_fusion), kind=kLoop, calls=%fused_computation.11 | loop fusion | flops 524288 | bytes 3145732 | tf_op jit(solution)/shard_map/while/body/eval_jaxpr/cond/branch_1_fun/dynamic_update_slice | solution.py:76
  86.8 0.1 select_reduce_fusion.3
  86.9 0.7 fusion.37
  88.8 7.9 %conditional.3 = ((f32[1024,128]{1,0:T(8,128)S(1)}, f32[4096,256]{1,0:T(8,128)})) conditional(s32[]{:T(128)} %convert_element_type.47, (f32[1024,128]{1,0:T(8,128)S(1)}, f32[4096,256]{1,0:T(8,128)}) %tuple.68, (s32[128]{0:T(128)S(1)}, s32[1024]{0:T(1024)S(1)}, s32[]{:T(128)}, bf16[4096,128]{1,0:T(8,128)(2,1)S(1)}, bf16[1024,128]{1,0:T(8,128)(2,1)S(1)}, ...), branch_computations={%region_6.6_spmd, %region_7.7_spmd} | conditional | flops 1355677696 | bytes 25985610 | solution.py:82
  88.8 0.7 fusion.11
  89.6 0.9 fusion.4
  90.5 2.3 %fusion.2 = bf16[1024,1024]{0,1:T(8,128)(2,1)S(1)} fusion(f32[1024,1024]{1,0:T(8,128)S(1)} %fusion.11, bf16[1024,128]{1,0:T(8,128)(2,1)S(1)} %get-tuple-element.413, f32[1024]{0:T(1024)S(1)} %bitcast.30, f32[1024]{0:T(1024)S(1)} %bitcast.33, s32[1024]{0:T(1024)S(1)} %broadcast_bitcast_fusion, s32[1024]{0:T(1024)S(1)} %get-tuple-element.407, ...), kind=kOutput, calls=%fused_computation.2 | convolution fusion | flops 275775488 | bytes 6832132 | tf_op jit(solution)/shard_map/while/body/eval_jaxpr/cond/branch_1_fun/dot_general | solution.py:62
  92.8 0.8 fusion.7
  93.6 0.7 convolution_multiply_fusion
  94.3 2.4 %fusion.8 = f32[4096,256]{1,0:T(8,128)} fusion(f32[4096,256]{1,0:T(8,128)} %get-tuple-element.415, s32[]{:T(128)S(6)} %select_n.88, f32[1024,128]{1,0:T(8,128)S(1)} %fusion.4, f32[1024,128]{1,0:T(8,128)S(1)} %convolution_multiply_fusion), kind=kLoop, calls=%fused_computation.11 | loop fusion | flops 524288 | bytes 3145732 | tf_op jit(solution)/shard_map/while/body/eval_jaxpr/cond/branch_1_fun/dynamic_update_slice | solution.py:76
  96.7 0.1 select_reduce_fusion.3
  96.8 0.7 fusion.37
  98.7 7.9 %conditional.3 = ((f32[1024,128]{1,0:T(8,128)S(1)}, f32[4096,256]{1,0:T(8,128)})) conditional(s32[]{:T(128)} %convert_element_type.47, (f32[1024,128]{1,0:T(8,128)S(1)}, f32[4096,256]{1,0:T(8,128)}) %tuple.68, (s32[128]{0:T(128)S(1)}, s32[1024]{0:T(1024)S(1)}, s32[]{:T(128)}, bf16[4096,128]{1,0:T(8,128)(2,1)S(1)}, bf16[1024,128]{1,0:T(8,128)(2,1)S(1)}, ...), branch_computations={%region_6.6_spmd, %region_7.7_spmd} | conditional | flops 1355677696 | bytes 25985610 | solution.py:82
  98.8 0.7 fusion.11
  99.5 0.9 fusion.4
  100.4 2.3 %fusion.2 = bf16[1024,1024]{0,1:T(8,128)(2,1)S(1)} fusion(f32[1024,1024]{1,0:T(8,128)S(1)} %fusion.11, bf16[1024,128]{1,0:T(8,128)(2,1)S(1)} %get-tuple-element.413, f32[1024]{0:T(1024)S(1)} %bitcast.30, f32[1024]{0:T(1024)S(1)} %bitcast.33, s32[1024]{0:T(1024)S(1)} %broadcast_bitcast_fusion, s32[1024]{0:T(1024)S(1)} %get-tuple-element.407, ...), kind=kOutput, calls=%fused_computation.2 | convolution fusion | flops 275775488 | bytes 6832132 | tf_op jit(solution)/shard_map/while/body/eval_jaxpr/cond/branch_1_fun/dot_general | solution.py:62
  102.7 0.8 fusion.7
  103.5 0.7 convolution_multiply_fusion
  104.2 2.3 %fusion.8 = f32[4096,256]{1,0:T(8,128)} fusion(f32[4096,256]{1,0:T(8,128)} %get-tuple-element.415, s32[]{:T(128)S(6)} %select_n.88, f32[1024,128]{1,0:T(8,128)S(1)} %fusion.4, f32[1024,128]{1,0:T(8,128)S(1)} %convolution_multiply_fusion), kind=kLoop, calls=%fused_computation.11 | loop fusion | flops 524288 | bytes 3145732 | tf_op jit(solution)/shard_map/while/body/eval_jaxpr/cond/branch_1_fun/dynamic_update_slice | solution.py:76
  106.7 49.7 %reduce-scatter.3.cloned.1.call-done = f32[512,256]{1,0:T(8,128)} async-done(((f32[4096,256]{1,0:T(8,128)}), f32[512,256]{1,0:T(8,128)}) %reduce-scatter.3.cloned.1.call-update) | async-done | bytes 524304 | tf_op jit(solution)/shard_map/reduce_scatter | solution.py:85
  156.4 0.7 convert_element_type.38
  157.2 24.9 %reduce-scatter.5.cloned.1.call-done = f32[128,256]{1,0:T(8,128)} async-done(((f32[512,256]{1,0:T(8,128)}), f32[128,256]{1,0:T(8,128)}) %reduce-scatter.5.cloned.1.call-update) | async-done | bytes 131088 | tf_op jit(solution)/shard_map/reduce_scatter | solution.py:86
  182.1 0.9 convert.4
  183.0 0.6 fusion.29
  (30 shorter events, 0.6 us)
Async XLA Ops:
  7.2 59.7 %copy-start.3 = (s32[64]{0:T(128)S(1)}, s32[64]{0:T(128)}, u32[]{:S(2)}) copy-start(s32[64]{0:T(128)} %param.17) | copy-start | bytes 772
  7.2 59.7 %copy-start.2 = (bf16[8,128,128]{2,1,0:T(8,128)(2,1)S(1)}, bf16[8,128,128]{2,1,0:T(8,128)(2,1)}, u32[]{:S(2)}) copy-start(bf16[8,128,128]{2,1,0:T(8,128)(2,1)} %param.15) | copy-start | bytes 786436
  7.2 59.7 %copy-start.4 = (f32[8,128]{1,0:T(8,128)S(1)}, f32[8,128]{1,0:T(8,128)}, u32[]{:S(2)}) copy-start(f32[8,128]{1,0:T(8,128)} %param.16) | copy-start | bytes 12292
  7.2 59.7 %copy-start = (bf16[8,128,128]{2,1,0:T(8,128)(2,1)S(1)}, bf16[8,128,128]{2,1,0:T(8,128)(2,1)}, u32[]{:S(2)}) copy-start(bf16[8,128,128]{2,1,0:T(8,128)(2,1)} %param.11) | copy-start | bytes 786436
  7.2 34.1 %all-gather.3.cloned.1.call-start = ((), (), s32[]{:S(2)}) async-start(), calls=%async_computation.2 | async-start | bytes 1179648 | tf_op jit(solution)/shard_map/all_gather | solution.py:43
  18.8 45.9 %all-gather.5.cloned.1.call-start = ((), (), s32[]{:S(2)}) async-start(), calls=%async_computation.3 | async-start | bytes 1179648 | tf_op jit(solution)/shard_map/all_gather | solution.py:44
  27.8 128.6 %reduce-scatter.3.cloned.1.call-start = ((), (), s32[]{:S(2)}) async-start(), calls=%async_computation.4 | async-start | bytes 4718592 | tf_op jit(solution)/shard_map/reduce_scatter | solution.py:85
  41.3 25.6 %copy-start.1 = (bf16[4096,128]{1,0:T(8,128)(2,1)S(1)}, bf16[4096,128]{1,0:T(8,128)(2,1)}, u32[]{:S(2)}) copy-start(bf16[4096,128]{1,0:T(8,128)(2,1)} %all-gather.3.cloned.1.call-done) | copy-start | bytes 3145732
  106.6 75.4 %reduce-scatter.5.cloned.1.call-start = ((), (), s32[]{:S(2)}) async-start(), calls=%async_computation.5 | async-start | bytes 655360 | tf_op jit(solution)/shard_map/reduce_scatter | solution.py:86
Sparse Core Ops, SparseCore 0:
  18.9 22.3 all-gather.2
  42.9 21.7 all-gather.4
  106.7 49.6 reduce-scatter.2
  159.1 22.9 reduce-scatter.4
where the time goes:
time: 191 us; the launch traced here: 190 us
  waiting for transfers between devices  109 us (57%)
  matrix products  21.8 us (11%)
  blocking collectives  20.4 us (11%)
  other arithmetic  16.8 us (9%)
  between operations  13.8 us (7%)
  loops' own time  5.31 us (3%)
  local copies, waits for them, and re-layouts  2.92 us (2%)
    reduce_scatter x1, waiting for transfers between devices, body(): lax.psum_scatter(grad_keys, 'outer', scatter_dimension=0, tiled=True)  49.7 us
    reduce_scatter x1, waiting for transfers between devices, body(): lax.psum_scatter(group_part, 'inner', scatter_dimension=0, tiled=True)  24.9 us
    all_gather x1, waiting for transfers between devices, body(): value_piece = lax.all_gather(group_value, 'outer', axis=0, tiled=True)  23.4 us
    all_gather x1, blocking collectives, body(): lax.all_gather(key_states, 'inner', axis=0, tiled=True)  11.5 us
    all_gather x1, waiting for transfers between devices, body(): key_piece = lax.all_gather(group_key, 'outer', axis=0, tiled=True)  10.8 us
    dynamic_update_slice x4, other arithmetic, compute(): lax.dynamic_update_slice_in_dim(grad_keys, updated, local_start, 0)  9.4 us
    dot_general x4, matrix products, compute(): jnp.dot(grad_rows, value_block.T, preferred_element_type=jnp.float32)  9.15 us
    all_gather x1, blocking collectives, body(): lax.all_gather(value_states, 'inner', axis=0, tiled=True)  8.92 us
  transfers between devices with their start and end apart: 4, of which 4 were waited for; matrix products, arithmetic and copies ran while one was open for 2% of the time, Pallas kernels for 0%

commit v1 on v0

v1 whole, which is shorter than its diff:
```python
import functools
import math

import jax
import jax.numpy as jnp
from jax import lax
from jax.experimental import pallas as pl
from jax.experimental.pallas import tpu as pltpu
from jax.sharding import PartitionSpec as P

MESH = pl.DeviceIdType.MESH
F32 = jnp.float32
BF16 = jnp.bfloat16
LOG2E = math.log2(math.e)


def dot(a, b, dims, precision=None):
    return lax.dot_general(
        a, b, ((dims[:1], dims[1:]), ((), ())), precision=precision, preferred_element_type=F32
    )


def kernel(
    planes, inner,
    order, q_ref, k_ref, v_ref, o_ref, g_ref, lse_ref,
    dq_out, dk_out, dv_out,
    kv, q2, g2, stats, low_pos, dq_acc, dq_send, dq_recv,
    diag, full, own, part_send, part_recv, z_send, z_recv,
    s_outer, s_inner, r_kv, s_q, r_q, s_part, r_part, s_z, r_z, s_dq, r_dq,
):
    heads, rows, width = q_ref.shape
    span = rows // 2
    cols = heads * span
    scale = 1.0 / math.sqrt(width)
    outer_id = lax.axis_index("outer")
    i = lax.axis_index("inner")
    core = lax.rem(outer_id, 2)
    z = outer_id // 2
    partner = (outer_id + 1 - 2 * core, i)

    def plane_of(step):
        return lax.rem(z + step, planes)

    def peer_of(step):
        return lax.rem(i + step, inner)

    def column(plane):
        return (plane * 2 + core, i)

    def beside(peer):
        return (outer_id, peer)

    def rank(plane, peer):
        return (plane * 2 + core) * inner + peer

    barrier = pltpu.get_barrier_semaphore()
    for step in range(1, planes):
        pl.semaphore_signal(barrier, inc=1, device_id=column(plane_of(step)), device_id_type=MESH)
    for step in range(1, inner):
        pl.semaphore_signal(barrier, inc=1, device_id=beside(peer_of(step)), device_id_type=MESH)
    pl.semaphore_signal(barrier, inc=1, device_id=partner, device_id_type=MESH)

    my_rank = outer_id * inner + i
    first = order[2 * my_rank]
    second = order[2 * my_rank + 1]

    def ordered(a, b):
        shape = a.shape
        straight = jnp.full(shape, first, jnp.int32) < jnp.full(shape, second, jnp.int32)
        a, b = a.astype(F32), b.astype(F32)
        return jnp.where(straight, a, b), jnp.where(straight, b, a)

    my_low = jnp.minimum(first, second)
    other_rank = partner[0] * inner + i
    other_low = jnp.minimum(order[2 * other_rank], order[2 * other_rank + 1])

    def kv_slot(plane, peer):
        return kv.at[plane, :, pl.ds(pl.multiple_of(peer * span, span), span), :]

    k_low, k_high = (x.astype(BF16) for x in ordered(k_ref[:span, :], k_ref[span:, :]))
    v_low, v_high = (x.astype(BF16) for x in ordered(v_ref[:span, :], v_ref[span:, :]))
    mine = pl.ds(pl.multiple_of(i * span, span), span)
    kv[z, 0, mine, :width] = k_low
    kv[z, 0, mine, width:] = v_low
    kv[z, 1, mine, :width] = k_high
    kv[z, 1, mine, width:] = v_high

    pl.semaphore_wait(barrier, planes + inner - 1)

    def send_column(step):
        return pltpu.make_async_remote_copy(
            src_ref=kv_slot(z, i), dst_ref=kv_slot(z, i),
            send_sem=s_outer.at[step], recv_sem=r_kv.at[z, i],
            device_id=column(plane_of(step)), device_id_type=MESH,
        )

    def send_beside(plane, step):
        return pltpu.make_async_remote_copy(
            src_ref=kv_slot(plane, i), dst_ref=kv_slot(plane, i),
            send_sem=s_inner.at[plane, step], recv_sem=r_kv.at[plane, i],
            device_id=beside(peer_of(step)), device_id_type=MESH,
        )

    def wait_kv(plane, peer):
        pltpu.make_async_remote_copy(
            src_ref=kv_slot(plane, peer), dst_ref=kv_slot(plane, peer),
            send_sem=s_outer.at[0], recv_sem=r_kv.at[plane, peer],
            device_id=partner, device_id_type=MESH,
        ).wait_recv()

    for step in range(1, planes):
        send_column(step).start()
    for step in range(1, inner):
        send_beside(z, step).start()

    def flat(ref):
        first_part = ref[:, :span, :].reshape(cols, width)
        return ordered(first_part, ref[:, span:, :].reshape(cols, width))

    g_wide = flat(g_ref)
    g_low, g_high = (x.astype(BF16) for x in g_wide)
    g2[0, :, :width] = g_low
    g2[0, :, width:] = g_high
    q_low, q_high = (x.astype(BF16) for x in flat(q_ref))
    q2[0, :, :width] = q_low
    q2[0, :, width:] = q_high

    def exchange(ref, index):
        return pltpu.make_async_remote_copy(
            src_ref=ref.at[0], dst_ref=ref.at[1], send_sem=s_q.at[index], recv_sem=r_q.at[index],
            device_id=partner, device_id_type=MESH,
        )

    exchange(q2, 0).start()
    exchange(g2, 1).start()
    ones = jnp.ones((8, width), F32)
    lse_first = jnp.concatenate([lse_ref[h : h + 1, :span] for h in range(heads)], axis=1) * LOG2E
    lse_second = jnp.concatenate([lse_ref[h : h + 1, span:] for h in range(heads)], axis=1) * LOG2E
    stats[0, 0:1, :], stats[0, 1:2, :] = ordered(lse_first, lse_second)
    for at, g_part, o_part in zip((2, 3), g_wide, flat(o_ref)):
        product = g_part * o_part
        stats[0, at : at + 1, :] = dot(ones, product, (1, 1), lax.Precision.HIGHEST)[0:1]
    stats[0, 4:8, :] = jnp.zeros((4, cols), F32)
    exchange(stats, 2).start()

    for step in range(1, planes):
        plane = plane_of(step)
        wait_kv(plane, i)
        for hop in range(1, inner):
            send_beside(plane, hop).start()

    key_row = lax.broadcasted_iota(jnp.int32, (span, cols), 0)
    query_row = lax.rem(lax.broadcasted_iota(jnp.int32, (span, cols), 1), span)
    visible = query_row >= key_row
    for half, k_part, v_part, q_part, g_part in (
        (0, k_low, v_low, q_low, g_low), (1, k_high, v_high, q_high, g_high),
    ):
        scores = dot(k_part, q_part, (1, 1)) * (scale * LOG2E)
        attend = jnp.where(visible, jnp.exp2(scores - stats[0, half : half + 1, :]), 0.0)
        grad = dot(v_part, g_part, (1, 1)) - stats[0, 2 + half : 3 + half, :]
        score_low = (attend * grad).astype(BF16)
        diag[half, :, :width] = dot(score_low, q_part, (1, 0))
        diag[half, :, width:] = dot(attend.astype(BF16), g_part, (1, 0))
        dq_acc[0, half * width : (half + 1) * width, :] = dot(k_part, score_low, (0, 0))
    dq_acc[1] = jnp.zeros((2 * width, cols), F32)

    for plane in range(planes):
        for peer in range(inner):
            at = 2 * rank(plane, peer)
            low = jnp.minimum(order[at], order[at + 1])
            low_pos[plane, peer * span : (peer + 1) * span, :] = jnp.full((span, width), low, jnp.int32)

    for index, ref in enumerate((q2, g2, stats)):
        exchange(ref, index).wait_recv()

    def send_part(plane, step):
        peer = peer_of(step)
        return pltpu.make_async_remote_copy(
            src_ref=part_send.at[plane, :, pl.ds(pl.multiple_of(peer * span, span), span), :],
            dst_ref=part_recv.at[plane, i],
            send_sem=s_part.at[plane, step], recv_sem=r_part.at[plane, i],
            device_id=beside(peer), device_id_type=MESH,
        )

    def gather_part(plane):
        total = own[plane]
        for step in range(1, inner):
            peer = peer_of(step)
            pltpu.make_async_remote_copy(
                src_ref=part_recv.at[plane, peer], dst_ref=part_recv.at[plane, peer],
                send_sem=s_part.at[plane, 0], recv_sem=r_part.at[plane, peer],
                device_id=partner, device_id_type=MESH,
            ).wait_recv()
            total = total + part_recv[plane, peer].astype(F32)
        return total

    def send_plane(step):
        plane = plane_of(step)
        return pltpu.make_async_remote_copy(
            src_ref=z_send.at[plane], dst_ref=z_recv.at[z],
            send_sem=s_z.at[step], recv_sem=r_z.at[z],
            device_id=column(plane), device_id_type=MESH,
        )

    def pass_on(step):
        plane = plane_of(step)
        z_send[plane] = gather_part(plane).astype(BF16)
        send_plane(step).start()

    def one_plane(step, carried):
        plane = plane_of(step)
        for hop in range(1, inner):
            wait_kv(plane, peer_of(hop))
        k_l, v_l = kv[plane, 0, :, :width], kv[plane, 0, :, width:]
        k_h, v_h = kv[plane, 1, :, :width], kv[plane, 1, :, width:]
        pos = low_pos[plane]
        wide_pos = jnp.concatenate([pos] * (cols // width), axis=1)
        dk_l = dv_l = dk_h = dv_h = None
        for j, edge in ((0, my_low), (1, other_low)):
            def below(x):
                return jnp.where(pos < edge, x, 0.0)

            def above(x):
                return jnp.where(pos > edge, x, 0.0)

            def chosen(low, high):
                low, high = below(low.astype(F32)), above(high.astype(F32))
                return jnp.concatenate([low.astype(BF16), high.astype(BF16)], axis=1)

            q_both, g_both = q2[j], g2[j]
            q_h, g_h = q_both[:, width:], g_both[:, width:]
            lse_l, lse_h = stats[j, 0:1, :], stats[j, 1:2, :]
            del_l, del_h = stats[j, 2:3, :], stats[j, 3:4, :]
            attend = jnp.exp2(dot(k_l, q_h, (1, 1)) * (scale * LOG2E) - lse_h)
            score_low = (attend * (dot(v_l, g_h, (1, 1)) - del_h)).astype(BF16)
            dv1 = dot(attend.astype(BF16), g_h, (1, 0))
            dk1 = dot(score_low, q_h, (1, 0))
            dq_acc[j, width:, :] += dot(k_l, score_low, (0, 0))
            is_below = wide_pos < edge
            k_c, v_c = chosen(k_l, k_h), chosen(v_l, v_h)
            attend = jnp.exp2(
                dot(k_c, q_both, (1, 1)) * (scale * LOG2E) - jnp.where(is_below, lse_l, lse_h)
            )
            grad = dot(v_c, g_both, (1, 1)) - jnp.where(is_below, del_l, del_h)
            score_low = (attend * grad).astype(BF16)
            dv2 = dot(attend.astype(BF16), g_both, (1, 0))
            dk2 = dot(score_low, q_both, (1, 0))
            dq_acc[j] += dot(k_c, score_low, (0, 0))
            dk_lj, dk_hj = dk1 + below(dk2[:, :width]), above(dk2[:, width:])
            dv_lj, dv_hj = dv1 + below(dv2[:, :width]), above(dv2[:, width:])
            if j == 0:
                dk_l, dk_h, dv_l, dv_h = dk_lj, dk_hj, dv_lj, dv_hj
            else:
                dk_l, dk_h, dv_l, dv_h = dk_l + dk_lj, dk_h + dk_hj, dv_l + dv_lj, dv_h + dv_hj
        for half, dk, dv in ((0, dk_l, dv_l), (1, dk_h, dv_h)):
            full[half, :, :width] = dk
            full[half, :, width:] = dv
            part_send[plane, half, :, :width] = dk.astype(BF16)
            part_send[plane, half, :, width:] = dv.astype(BF16)
        own[plane] = full[:, mine, :]
        for hop in range(1, inner):
            send_part(plane, hop).start()

        @pl.when(step >= 2)
        def _():
            pass_on(step - 1)

        return carried

    lax.fori_loop(0, planes, one_plane, 0)

    dq_send[...] = dq_acc[1].astype(BF16)
    dq_copy = pltpu.make_async_remote_copy(
        src_ref=dq_send, dst_ref=dq_recv, send_sem=s_dq, recv_sem=r_dq,
        device_id=partner, device_id_type=MESH,
    )
    dq_copy.start()
    pass_on(planes - 1)

    dq_copy.wait_recv()
    dq = (dq_acc[0] + dq_recv[...].astype(F32)) * scale
    for at, part in zip((0, span), ordered(dq[:width], dq[width:])):
        dq_out[:, at : at + span, :] = part.T.astype(BF16).reshape(heads, span, width)

    total = gather_part(z) + diag[...]
    for step in range(1, planes):
        plane = plane_of(step)
        pltpu.make_async_remote_copy(
            src_ref=z_recv.at[plane], dst_ref=z_recv.at[plane],
            send_sem=s_z.at[0], recv_sem=r_z.at[plane],
            device_id=partner, device_id_type=MESH,
        ).wait_recv()
        total = total + z_recv[plane].astype(F32)
    for at, part in zip((0, span), ordered(total[0], total[1])):
        dk_out[at : at + span, :] = (part[:, :width] * scale).astype(BF16)
        dv_out[at : at + span, :] = part[:, width:].astype(BF16)

    for step in range(1, planes):
        send_column(step).wait_send()
        send_plane(step).wait_send()
    for step in range(planes):
        for hop in range(1, inner):
            send_beside(plane_of(step), hop).wait_send()
            send_part(plane_of(step), hop).wait_send()
    for index, ref in enumerate((q2, g2, stats)):
        exchange(ref, index).wait_send()
    dq_copy.wait_send()


def body(queries, key_states, value_states, outputs, grad_outputs, log_sums, span_order):
    heads, rows, width = queries.shape
    planes = lax.axis_size("outer") // 2
    inner = lax.axis_size("inner")
    span = rows // 2
    cols = heads * span
    group = inner * span
    vmem = pl.BlockSpec(memory_space=pltpu.VMEM)
    dma = pltpu.SemaphoreType.DMA
    return pl.pallas_call(
        functools.partial(kernel, planes, inner),
        out_shape=(
            jax.ShapeDtypeStruct(queries.shape, BF16),
            jax.ShapeDtypeStruct(key_states.shape, BF16),
            jax.ShapeDtypeStruct(value_states.shape, BF16),
        ),
        in_specs=[pl.BlockSpec(memory_space=pltpu.SMEM)] + [vmem] * 6,
        out_specs=(vmem, vmem, vmem),
        scratch_shapes=[
            pltpu.VMEM((planes, 2, group, 2 * width), BF16),
            pltpu.VMEM((2, cols, 2 * width), BF16),
            pltpu.VMEM((2, cols, 2 * width), BF16),
            pltpu.VMEM((2, 8, cols), F32),
            pltpu.VMEM((planes, group, width), jnp.int32),
            pltpu.VMEM((2, 2 * width, cols), F32),
            pltpu.VMEM((2 * width, cols), BF16),
            pltpu.VMEM((2 * width, cols), BF16),
            pltpu.VMEM((2, span, 2 * width), F32),
            pltpu.VMEM((2, group, 2 * width), F32),
            pltpu.VMEM((planes, 2, span, 2 * width), F32),
            pltpu.VMEM((planes, 2, group, 2 * width), BF16),
            pltpu.VMEM((planes, inner, 2, span, 2 * width), BF16),
            pltpu.VMEM((planes, 2, span, 2 * width), BF16),
            pltpu.VMEM((planes, 2, span, 2 * width), BF16),
            dma((planes,)), dma((planes, inner)), dma((planes, inner)),
            dma((3,)), dma((3,)),
            dma((planes, inner)), dma((planes, inner)),
            dma((planes,)), dma((planes,)),
            dma, dma,
        ],
        compiler_params=pltpu.CompilerParams(
            collective_id=0, has_side_effects=True, vmem_limit_bytes=48 * 1024 * 1024
        ),
        cost_estimate=pl.CostEstimate(
            flops=10 * 65 * cols * span * width * planes * inner // 16,
            bytes_accessed=4 * heads * rows * width * 2,
            transcendentals=0,
        ),
    )(span_order, queries, key_states, value_states, outputs, grad_outputs, log_sums)


def solution(mesh):
    return jax.shard_map(
        body,
        mesh=mesh,
        in_specs=(
            P(None, ("outer", "inner"), None),
            P(("outer", "inner"), None),
            P(("outer", "inner"), None),
            P(None, ("outer", "inner"), None),
            P(None, ("outer", "inner"), None),
            P(None, ("outer", "inner")),
            P(),
        ),
        out_specs=(
            P(None, ("outer", "inner"), None),
            P(("outer", "inner"), None),
            P(("outer", "inner"), None),
        ),
        check_vma=False,
    )
```

time: 191 us -> 48.2 us (0.25)
  waiting for transfers between devices: 109 us -> 0 us
  Pallas kernels: 0 us -> 39.6 us
  matrix products: 21.8 us -> 0 us
  blocking collectives: 20.4 us -> 0 us
  other arithmetic: 16.8 us -> 0 us
  between operations: 13.8 us -> 0.66 us
  loops' own time: 5.31 us -> 0 us
  local copies, waits for them, and re-layouts: 2.92 us -> 7.63 us
    reduce_scatter x2 -> x0, waiting for transfers between devices: 74.6 us -> none  [the longest x1 49.7 us: body(): lax.psum_scatter(grad_keys, 'outer', scatter_dimension=0, tiled=True)]
    pallas_call x0 -> x1, Pallas kernels: none -> 39.6 us  [body(): pl.pallas_call(functools.partial(kernel, planes, inner), out_shape=(jax.S...]
    all_gather x2 -> x0, waiting for transfers between devices: 34.2 us -> none  [the longest x1 23.4 us: body(): value_piece = lax.all_gather(group_value, 'outer', axis=0, tiled=True)]
    dot_general x20 -> x0, matrix products: 21.8 us -> none  [the longest x4 9.15 us: compute(): jnp.dot(grad_rows, value_block.T, preferred_element_type=jnp.float32)]
    all_gather x2 -> x0, blocking collectives: 20.4 us -> none  [the longest x1 11.5 us: body(): lax.all_gather(key_states, 'inner', axis=0, tiled=True)]
    dynamic_update_slice x4 -> x0, other arithmetic: 9.4 us -> none  [compute(): lax.dynamic_update_slice_in_dim(grad_keys, updated, local_start, 0)]
    unnamed x10 -> x17, local copies, waits for them, and re-layouts: 0.02 us -> 7.63 us
    another operation x5 -> x0, loops' own time: 5.31 us -> none  [the longest x1 5.07 us: body(): lax.fori_loop(0, piece_rows // block_rows, one_block, initial)]
  transfers between devices with their start and end apart: 4 -> 0, of which waited for: 4 -> 0; matrix products, arithmetic and copies ran while one was open for 2% -> 0% of each run, Pallas kernels for 0% -> 0%
where the time goes in v1:
time: 48.2 us; the launch traced here: 47.8 us
  Pallas kernels  39.6 us (82%)
  local copies, waits for them, and re-layouts  7.63 us (16%)
  between operations  0.66 us (1%)
    pallas_call x1, Pallas kernels, body(): pl.pallas_call(functools.partial(kernel, planes, inner), out_shape=(jax.S...  39.6 us
    unnamed x17, local copies, waits for them, and re-layouts  7.63 us

profile of v1, /device:TPU:0, one launch (start us, length us, event | category | flops | bytes accessed | tf_op | source)
XLA Modules:
  0.0 47.8 jit_solution(13636395065735327810)
XLA Ops:
  0.6 0.0 copy-start
  0.6 0.9 %copy-done = bf16[8,128,128]{2,1,0:T(8,128)(2,1)S(1)} copy-done((bf16[8,128,128]{2,1,0:T(8,128)(2,1)S(1)}, bf16[8,128,128]{2,1,0:T(8,128)(2,1)}, u32[]{:S(2)}) %copy-start) | copy-done | bytes 262168
  1.6 0.0 copy-start.1
  1.6 0.9 %copy-done.1 = bf16[8,128,128]{2,1,0:T(8,128)(2,1)S(1)} copy-done((bf16[8,128,128]{2,1,0:T(8,128)(2,1)S(1)}, bf16[8,128,128]{2,1,0:T(8,128)(2,1)}, u32[]{:S(2)}) %copy-start.1) | copy-done | bytes 262168
  2.5 0.0 copy-start.2
  2.5 0.9 %copy-done.2 = bf16[8,128,128]{2,1,0:T(8,128)(2,1)S(1)} copy-done((bf16[8,128,128]{2,1,0:T(8,128)(2,1)S(1)}, bf16[8,128,128]{2,1,0:T(8,128)(2,1)}, u32[]{:S(2)}) %copy-start.2) | copy-done | bytes 262168
  3.5 0.0 copy-start.3
  3.5 0.8 %copy-done.3 = bf16[128,128]{1,0:T(8,128)(2,1)S(1)} copy-done((bf16[128,128]{1,0:T(8,128)(2,1)S(1)}, bf16[128,128]{1,0:T(8,128)(2,1)}, u32[]{:S(2)}) %copy-start.3) | copy-done | bytes 32792
  4.2 0.0 copy-start.4
  4.2 0.8 %copy-done.4 = bf16[128,128]{1,0:T(8,128)(2,1)S(1)} copy-done((bf16[128,128]{1,0:T(8,128)(2,1)S(1)}, bf16[128,128]{1,0:T(8,128)(2,1)}, u32[]{:S(2)}) %copy-start.4) | copy-done | bytes 32792
  5.0 0.0 copy-start.5
  5.0 0.7 %copy-done.5 = f32[8,128]{1,0:T(8,128)S(1)} copy-done((f32[8,128]{1,0:T(8,128)S(1)}, f32[8,128]{1,0:T(8,128)}, u32[]{:S(2)}) %copy-start.5) | copy-done | bytes 4120
  5.7 0.0 copy-start.6
  5.7 0.7 %copy-done.6 = s32[64]{0:T(128)S(1)} copy-done((s32[64]{0:T(128)S(1)}, s32[64]{0:T(128)}, u32[]{:S(2)}) %copy-start.6) | copy-done | bytes 280
  6.3 39.6 %shard_map.94 = (bf16[8,128,128]{2,1,0:T(8,128)(2,1)S(1)}, bf16[128,128]{1,0:T(8,128)(2,1)S(1)}, bf16[128,128]{1,0:T(8,128)(2,1)S(1)}) custom-call(s32[64]{0:T(128)S(1)} %copy-done.6, bf16[8,128,128]{2,1,0:T(8,128)(2,1)S(1)} %copy-done, bf16[128,128]{1,0:T(8,128)(2,1)S(1)} %copy-done.3, bf16[128,128]{1,0:T(8,128)(2,1)S(1)} %copy-done.4, ...), custom_call_target="tpu_custom_call" | custom-call | flops 2726297600 | bytes 1048576 | tf_op jit(solution)/shard_map/pallas_call | solution.py:319
  45.9 0.7 %copy.13 = bf16[8,128,128]{2,1,0:T(8,128)(2,1)} copy(bf16[8,128,128]{2,1,0:T(8,128)(2,1)S(1)} %get-tuple-element.6) | data formatting | bytes 524288
  46.6 0.6 %copy.14 = bf16[128,128]{1,0:T(8,128)(2,1)} copy(bf16[128,128]{1,0:T(8,128)(2,1)S(1)} %get-tuple-element.7) | data formatting | bytes 65536
  47.2 0.6 %copy.15 = bf16[128,128]{1,0:T(8,128)(2,1)} copy(bf16[128,128]{1,0:T(8,128)(2,1)S(1)} %get-tuple-element.8) | data formatting | bytes 65536
Async XLA Ops:
  0.6 1.0 %copy-start = (bf16[8,128,128]{2,1,0:T(8,128)(2,1)S(1)}, bf16[8,128,128]{2,1,0:T(8,128)(2,1)}, u32[]{:S(2)}) copy-start(bf16[8,128,128]{2,1,0:T(8,128)(2,1)} %q_ref.1) | copy-start | bytes 786436
  1.6 0.9 %copy-start.1 = (bf16[8,128,128]{2,1,0:T(8,128)(2,1)S(1)}, bf16[8,128,128]{2,1,0:T(8,128)(2,1)}, u32[]{:S(2)}) copy-start(bf16[8,128,128]{2,1,0:T(8,128)(2,1)} %o_ref.1) | copy-start | bytes 786436
  2.5 0.9 %copy-start.2 = (bf16[8,128,128]{2,1,0:T(8,128)(2,1)S(1)}, bf16[8,128,128]{2,1,0:T(8,128)(2,1)}, u32[]{:S(2)}) copy-start(bf16[8,128,128]{2,1,0:T(8,128)(2,1)} %g_ref.1) | copy-start | bytes 786436
  3.5 0.8 %copy-start.3 = (bf16[128,128]{1,0:T(8,128)(2,1)S(1)}, bf16[128,128]{1,0:T(8,128)(2,1)}, u32[]{:S(2)}) copy-start(bf16[128,128]{1,0:T(8,128)(2,1)} %k_ref.1) | copy-start | bytes 98308
  4.2 0.8 %copy-start.4 = (bf16[128,128]{1,0:T(8,128)(2,1)S(1)}, bf16[128,128]{1,0:T(8,128)(2,1)}, u32[]{:S(2)}) copy-start(bf16[128,128]{1,0:T(8,128)(2,1)} %v_ref.1) | copy-start | bytes 98308
  5.0 0.7 %copy-start.5 = (f32[8,128]{1,0:T(8,128)S(1)}, f32[8,128]{1,0:T(8,128)}, u32[]{:S(2)}) copy-start(f32[8,128]{1,0:T(8,128)} %lse_ref.1) | copy-start | bytes 12292
  5.7 0.7 %copy-start.6 = (s32[64]{0:T(128)S(1)}, s32[64]{0:T(128)}, u32[]{:S(2)}) copy-start(s32[64]{0:T(128)} %order.1) | copy-start | bytes 772

commit v2 on v1

--- a/solution.py
+++ b/solution.py
@@ -22,11 +22,12 @@
 
 def kernel(
     planes, inner,
-    order, q_ref, k_ref, v_ref, o_ref, g_ref, lse_ref,
+    order_hbm, q_hbm, k_hbm, v_hbm, o_hbm, g_hbm, lse_hbm,
     dq_out, dk_out, dv_out,
     kv, q2, g2, stats, low_pos, dq_acc, dq_send, dq_recv,
     diag, full, own, part_send, part_recv, z_send, z_recv,
-    s_outer, s_inner, r_kv, s_q, r_q, s_part, r_part, s_z, r_z, s_dq, r_dq,
+    order, q_ref, k_ref, v_ref, o_ref, g_ref, lse_ref, loads,
+    s_outer, s_inner, r_kv, s_cross, r_cross, s_q, r_q, s_part, r_part, s_z, r_z, s_dq, r_dq,
 ):
     heads, rows, width = q_ref.shape
     span = rows // 2
@@ -39,7 +40,18 @@
     partner = (outer_id + 1 - 2 * core, i)
 
     def plane_of(step):
-        return lax.rem(z + step, planes)
+        if planes & (planes - 1):
+            return lax.rem(z + step, planes)
+        plane, bit = 0, 1
+        while bit < planes:
+            plane = plane + bit * lax.rem(lax.div(z, bit) + lax.div(jnp.int32(step), jnp.int32(bit)), 2)
+            bit *= 2
+        return plane
+
+    side = lax.rem(i, 2)
+    across = i + 1 - 2 * side
+    along = [2 * lax.rem(i // 2 + t, inner // 2) + side for t in range(inner // 2)]
+    cross = [peer + 1 - 2 * side for peer in along]
 
     def peer_of(step):
         return lax.rem(i + step, inner)
@@ -52,6 +64,14 @@
 
     def rank(plane, peer):
         return (plane * 2 + core) * inner + peer
+
+    staged = (
+        (order_hbm, order), (k_hbm, k_ref), (v_hbm, v_ref), (g_hbm, g_ref), (q_hbm, q_ref),
+        (lse_hbm, lse_ref), (o_hbm, o_ref),
+    )
+    fetch = [pltpu.make_async_copy(a, b, loads.at[n]) for n, (a, b) in enumerate(staged)]
+    for one in fetch:
+        one.start()
 
     barrier = pltpu.get_barrier_semaphore()
     for step in range(1, planes):
@@ -60,6 +80,8 @@
         pl.semaphore_signal(barrier, inc=1, device_id=beside(peer_of(step)), device_id_type=MESH)
     pl.semaphore_signal(barrier, inc=1, device_id=partner, device_id_type=MESH)
 
+    for one in fetch[:3]:
+        one.wait()
     my_rank = outer_id * inner + i
     first = order[2 * my_rank]
     second = order[2 * my_rank + 1]
@@ -94,11 +116,22 @@
             device_id=column(plane_of(step)), device_id_type=MESH,
         )
 
-    def send_beside(plane, step):
+    def send_beside(plane, t):
         return pltpu.make_async_remote_copy(
             src_ref=kv_slot(plane, i), dst_ref=kv_slot(plane, i),
-            send_sem=s_inner.at[plane, step], recv_sem=r_kv.at[plane, i],
-            device_id=beside(peer_of(step)), device_id_type=MESH,
+            send_sem=s_inner.at[plane, t], recv_sem=r_kv.at[plane, i],
+            device_id=beside(along[t] if t else across), device_id_type=MESH,
+        )
+
+    def half_slot(plane, peer, half):
+        return kv.at[plane, half, pl.ds(pl.multiple_of(peer * span, span), span), :]
+
+    def send_cross(plane, t, half):
+        source, target = (across, along[t]) if half == 0 else (along[t], across)
+        return pltpu.make_async_remote_copy(
+            src_ref=half_slot(plane, source, half), dst_ref=half_slot(plane, source, half),
+            send_sem=s_cross.at[plane, t, half], recv_sem=r_cross.at[plane, source, half],
+            device_id=beside(target), device_id_type=MESH,
         )
 
     def wait_kv(plane, peer):
@@ -108,19 +141,41 @@
             device_id=partner, device_id_type=MESH,
         ).wait_recv()
 
+    def wait_cross(plane, peer, half):
+        pltpu.make_async_remote_copy(
+            src_ref=half_slot(plane, peer, half), dst_ref=half_slot(plane, peer, half),
+            send_sem=s_outer.at[0], recv_sem=r_cross.at[plane, peer, half],
+            device_id=partner, device_id_type=MESH,
+        ).wait_recv()
+
+    rows_of = range(1, inner // 2)
+
+    def spread(plane):
+        for t in range(inner // 2):
+            send_beside(plane, t).start()
+
+    def forward(plane):
+        wait_kv(plane, across)
+        for t in rows_of:
+            send_cross(plane, t, 0).start()
+        for t in rows_of:
+            wait_kv(plane, along[t])
+            send_cross(plane, t, 1).start()
+
     for step in range(1, planes):
         send_column(step).start()
-    for step in range(1, inner):
-        send_beside(z, step).start()
+    spread(z)
 
     def flat(ref):
         first_part = ref[:, :span, :].reshape(cols, width)
         return ordered(first_part, ref[:, span:, :].reshape(cols, width))
 
+    fetch[3].wait()
     g_wide = flat(g_ref)
     g_low, g_high = (x.astype(BF16) for x in g_wide)
     g2[0, :, :width] = g_low
     g2[0, :, width:] = g_high
+    fetch[4].wait()
     q_low, q_high = (x.astype(BF16) for x in flat(q_ref))
     q2[0, :, :width] = q_low
     q2[0, :, width:] = q_high
@@ -133,6 +188,8 @@
 
     exchange(q2, 0).start()
     exchange(g2, 1).start()
+    fetch[5].wait()
+    fetch[6].wait()
     ones = jnp.ones((8, width), F32)
     lse_first = jnp.concatenate([lse_ref[h : h + 1, :span] for h in range(heads)], axis=1) * LOG2E
     lse_second = jnp.concatenate([lse_ref[h : h + 1, span:] for h in range(heads)], axis=1) * LOG2E
@@ -144,10 +201,10 @@
     exchange(stats, 2).start()
 
     for step in range(1, planes):
-        plane = plane_of(step)
-        wait_kv(plane, i)
-        for hop in range(1, inner):
-            send_beside(plane, hop).start()
+        wait_kv(plane_of(step), i)
+        spread(plane_of(step))
+        if step == 1:
+            forward(z)
 
     key_row = lax.broadcasted_iota(jnp.int32, (span, cols), 0)
     query_row = lax.rem(lax.broadcasted_iota(jnp.int32, (span, cols), 1), span)
@@ -209,8 +266,9 @@
 
     def one_plane(step, carried):
         plane = plane_of(step)
-        for hop in range(1, inner):
-            wait_kv(plane, peer_of(hop))
+        for t in rows_of:
+            wait_cross(plane, cross[t], 0)
+            wait_cross(plane, cross[t], 1)
         k_l, v_l = kv[plane, 0, :, :width], kv[plane, 0, :, width:]
         k_h, v_h = kv[plane, 1, :, :width], kv[plane, 1, :, width:]
         pos = low_pos[plane]
@@ -250,6 +308,10 @@
             dv_lj, dv_hj = dv1 + below(dv2[:, :width]), above(dv2[:, width:])
             if j == 0:
                 dk_l, dk_h, dv_l, dv_h = dk_lj, dk_hj, dv_lj, dv_hj
+
+                @pl.when(step + 1 < planes)
+                def _():
+                    forward(plane_of(step + 1))
             else:
                 dk_l, dk_h, dv_l, dv_h = dk_l + dk_lj, dk_h + dk_hj, dv_l + dv_lj, dv_h + dv_hj
         for half, dk, dv in ((0, dk_l, dv_l), (1, dk_h, dv_h)):
@@ -300,8 +362,12 @@
         send_plane(step).wait_send()
     for step in range(planes):
         for hop in range(1, inner):
-            send_beside(plane_of(step), hop).wait_send()
             send_part(plane_of(step), hop).wait_send()
+        for t in range(inner // 2):
+            send_beside(plane_of(step), t).wait_send()
+        for t in rows_of:
+            send_cross(plane_of(step), t, 0).wait_send()
+            send_cross(plane_of(step), t, 1).wait_send()
     for index, ref in enumerate((q2, g2, stats)):
         exchange(ref, index).wait_send()
     dq_copy.wait_send()
@@ -323,7 +389,7 @@
             jax.ShapeDtypeStruct(key_states.shape, BF16),
             jax.ShapeDtypeStruct(value_states.shape, BF16),
         ),
-        in_specs=[pl.BlockSpec(memory_space=pltpu.SMEM)] + [vmem] * 6,
+        in_specs=[pl.BlockSpec(memory_space=pl.ANY)] * 7,
         out_specs=(vmem, vmem, vmem),
         scratch_shapes=[
             pltpu.VMEM((planes, 2, group, 2 * width), BF16),
@@ -341,7 +407,13 @@
             pltpu.VMEM((planes, inner, 2, span, 2 * width), BF16),
             pltpu.VMEM((planes, 2, span, 2 * width), BF16),
             pltpu.VMEM((planes, 2, span, 2 * width), BF16),
+            pltpu.SMEM(span_order.shape, jnp.int32),
+            pltpu.VMEM(queries.shape, BF16), pltpu.VMEM(key_states.shape, BF16),
+            pltpu.VMEM(value_states.shape, BF16), pltpu.VMEM(outputs.shape, BF16),
+            pltpu.VMEM(grad_outputs.shape, BF16), pltpu.VMEM(log_sums.shape, F32),
+            dma((7,)),
             dma((planes,)), dma((planes, inner)), dma((planes, inner)),
+            dma((planes, inner, 2)), dma((planes, inner, 2)),
             dma((3,)), dma((3,)),
             dma((planes, inner)), dma((planes, inner)),
             dma((planes,)), dma((planes,)),

time: 48.2 us -> 47.3 us (0.981)
  Pallas kernels: 39.6 us -> 38.6 us
    pallas_call x1, Pallas kernels: 39.6 us -> 38.6 us  [body(): pl.pallas_call(functools.partial(kernel, planes, inner), out_shape=(jax.S...]
where the time goes in v2:
time: 47.3 us; the launch traced here: 46.9 us
  Pallas kernels  38.6 us (82%)
  local copies, waits for them, and re-layouts  7.63 us (16%)
  between operations  0.66 us (1%)
    pallas_call x1, Pallas kernels, body(): pl.pallas_call(functools.partial(kernel, planes, inner), out_shape=(jax.S...  38.6 us
    unnamed x17, local copies, waits for them, and re-layouts  7.63 us

profile of v2, /device:TPU:0, one launch (start us, length us, event | category | flops | bytes accessed | tf_op | source)
XLA Modules:
  0.0 46.9 jit_solution(1064705626709731089)
XLA Ops:
  0.6 0.0 copy-start
  0.6 0.9 %copy-done = bf16[8,128,128]{2,1,0:T(8,128)(2,1)S(1)} copy-done((bf16[8,128,128]{2,1,0:T(8,128)(2,1)S(1)}, bf16[8,128,128]{2,1,0:T(8,128)(2,1)}, u32[]{:S(2)}) %copy-start) | copy-done | bytes 262168
  1.6 0.0 copy-start.1
  1.6 0.9 %copy-done.1 = bf16[8,128,128]{2,1,0:T(8,128)(2,1)S(1)} copy-done((bf16[8,128,128]{2,1,0:T(8,128)(2,1)S(1)}, bf16[8,128,128]{2,1,0:T(8,128)(2,1)}, u32[]{:S(2)}) %copy-start.1) | copy-done | bytes 262168
  2.5 0.0 copy-start.2
  2.5 0.9 %copy-done.2 = bf16[8,128,128]{2,1,0:T(8,128)(2,1)S(1)} copy-done((bf16[8,128,128]{2,1,0:T(8,128)(2,1)S(1)}, bf16[8,128,128]{2,1,0:T(8,128)(2,1)}, u32[]{:S(2)}) %copy-start.2) | copy-done | bytes 262168
  3.5 0.0 copy-start.3
  3.5 0.8 %copy-done.3 = bf16[128,128]{1,0:T(8,128)(2,1)S(1)} copy-done((bf16[128,128]{1,0:T(8,128)(2,1)S(1)}, bf16[128,128]{1,0:T(8,128)(2,1)}, u32[]{:S(2)}) %copy-start.3) | copy-done | bytes 32792
  4.2 0.0 copy-start.4
  4.2 0.8 %copy-done.4 = bf16[128,128]{1,0:T(8,128)(2,1)S(1)} copy-done((bf16[128,128]{1,0:T(8,128)(2,1)S(1)}, bf16[128,128]{1,0:T(8,128)(2,1)}, u32[]{:S(2)}) %copy-start.4) | copy-done | bytes 32792
  5.0 0.0 copy-start.5
  5.0 0.7 %copy-done.5 = f32[8,128]{1,0:T(8,128)S(1)} copy-done((f32[8,128]{1,0:T(8,128)S(1)}, f32[8,128]{1,0:T(8,128)}, u32[]{:S(2)}) %copy-start.5) | copy-done | bytes 4120
  5.7 0.0 copy-start.6
  5.7 0.7 %copy-done.6 = s32[64]{0:T(128)S(1)} copy-done((s32[64]{0:T(128)S(1)}, s32[64]{0:T(128)}, u32[]{:S(2)}) %copy-start.6) | copy-done | bytes 280
  6.3 38.6 %shard_map.94 = (bf16[8,128,128]{2,1,0:T(8,128)(2,1)S(1)}, bf16[128,128]{1,0:T(8,128)(2,1)S(1)}, bf16[128,128]{1,0:T(8,128)(2,1)S(1)}) custom-call(s32[64]{0:T(128)S(1)} %copy-done.6, bf16[8,128,128]{2,1,0:T(8,128)(2,1)S(1)} %copy-done, bf16[128,128]{1,0:T(8,128)(2,1)S(1)} %copy-done.3, bf16[128,128]{1,0:T(8,128)(2,1)S(1)} %copy-done.4, ...), custom_call_target="tpu_custom_call" | custom-call | flops 2726297600 | bytes 1048576 | tf_op jit(solution)/shard_map/pallas_call | solution.py:385
  45.0 0.7 %copy.13 = bf16[8,128,128]{2,1,0:T(8,128)(2,1)} copy(bf16[8,128,128]{2,1,0:T(8,128)(2,1)S(1)} %get-tuple-element.6) | data formatting | bytes 524288
  45.7 0.6 %copy.14 = bf16[128,128]{1,0:T(8,128)(2,1)} copy(bf16[128,128]{1,0:T(8,128)(2,1)S(1)} %get-tuple-element.7) | data formatting | bytes 65536
  46.3 0.6 %copy.15 = bf16[128,128]{1,0:T(8,128)(2,1)} copy(bf16[128,128]{1,0:T(8,128)(2,1)S(1)} %get-tuple-element.8) | data formatting | bytes 65536
Async XLA Ops:
  0.6 1.0 %copy-start = (bf16[8,128,128]{2,1,0:T(8,128)(2,1)S(1)}, bf16[8,128,128]{2,1,0:T(8,128)(2,1)}, u32[]{:S(2)}) copy-start(bf16[8,128,128]{2,1,0:T(8,128)(2,1)} %q_hbm.1) | copy-start | bytes 786436
  1.6 0.9 %copy-start.1 = (bf16[8,128,128]{2,1,0:T(8,128)(2,1)S(1)}, bf16[8,128,128]{2,1,0:T(8,128)(2,1)}, u32[]{:S(2)}) copy-start(bf16[8,128,128]{2,1,0:T(8,128)(2,1)} %o_hbm.1) | copy-start | bytes 786436
  2.5 0.9 %copy-start.2 = (bf16[8,128,128]{2,1,0:T(8,128)(2,1)S(1)}, bf16[8,128,128]{2,1,0:T(8,128)(2,1)}, u32[]{:S(2)}) copy-start(bf16[8,128,128]{2,1,0:T(8,128)(2,1)} %g_hbm.1) | copy-start | bytes 786436
  3.5 0.8 %copy-start.3 = (bf16[128,128]{1,0:T(8,128)(2,1)S(1)}, bf16[128,128]{1,0:T(8,128)(2,1)}, u32[]{:S(2)}) copy-start(bf16[128,128]{1,0:T(8,128)(2,1)} %k_hbm.1) | copy-start | bytes 98308
  4.2 0.8 %copy-start.4 = (bf16[128,128]{1,0:T(8,128)(2,1)S(1)}, bf16[128,128]{1,0:T(8,128)(2,1)}, u32[]{:S(2)}) copy-start(bf16[128,128]{1,0:T(8,128)(2,1)} %v_hbm.1) | copy-start | bytes 98308
  5.0 0.7 %copy-start.5 = (f32[8,128]{1,0:T(8,128)S(1)}, f32[8,128]{1,0:T(8,128)}, u32[]{:S(2)}) copy-start(f32[8,128]{1,0:T(8,128)} %lse_hbm.1) | copy-start | bytes 12292
  5.7 0.7 %copy-start.6 = (s32[64]{0:T(128)S(1)}, s32[64]{0:T(128)}, u32[]{:S(2)}) copy-start(s32[64]{0:T(128)} %order_hbm.1) | copy-start | bytes 772
